TPU v7x, 128 devices: a whole 4x4x4 slice. The times are simulated.
128 devices in a mesh: pair: 32 (over x, y, core), red: 4 (over z).
Axes of the slice: x: 4, y: 4, z: 4, core: 2. Of those that a mesh axis runs over, the one named last changes fastest.
Arguments:
- amplitudes: float32 [1024, 16, 9216], P('pair', None, 'red'), may hold values from -6 to 6
- tile_occ: int32 [1024], P('pair'), may hold values from 0 to 3
- tile_virt: int32 [1024, 1], P('pair'), may hold values from 0 to 31; in each aligned block of 32 rows (0 to 31, 32 to 63, ...) at most 2 rows name the same one
- owner: int32 [32], replicated, may hold values from 0 to 31, each once
- integrals: float32 [32, 9216, 1536], P('pair', 'red'), may hold values from -0.0625 to 0.0625
Outputs:
- residual: float32 [128, 16, 1536], P('pair', None, 'red')
Inputs may be any that keep to these rules, and one draw needn't show every extreme that they name: `tile_virt`: among the 32 tiles of one device, no virtual-pair tile is named more than 2 times, and in every draw some is named exactly 2 times. `owner`: each index of pair holds exactly one virtual-pair tile's integrals.
All inputs are finite; a program needn't handle non-finite values.
Results may differ from a plain program's by a relative error of at most 0.0001.
Values sent between devices are 32-bit elements; how exact they have to be, the bound alone decides.
A program may use at most 128 MiB of HBM per device.

v0:
```python
import jax
import jax.numpy as jnp
from jax import lax
from jax.sharding import PartitionSpec as P

OBLK = 4
CAP = 2


def shards(amplitudes, tile_occ, tile_virt, owner, integrals):
    peers = lax.axis_size("pair")
    slots, rows, inner = amplitudes.shape
    block = integrals[0]
    columns = block.shape[1]
    target = owner[tile_virt[:, 0]]
    order_ids = jnp.arange(slots, dtype=jnp.int32)
    earlier = (target[:, None] == target[None, :]) & (order_ids[None, :] < order_ids[:, None])
    place = jnp.sum(earlier.astype(jnp.int32), axis=1)
    outgoing = jnp.zeros((peers, CAP, rows, inner), jnp.float32).at[target, place].set(amplitudes)
    received = lax.all_to_all(outgoing, "pair", split_axis=0, concat_axis=0, tiled=True)
    sources = received.shape[0]
    items = received.shape[1]
    flat = received.reshape(sources * items * rows, inner)
    product = jnp.dot(
        flat, block, precision=lax.Precision.HIGHEST, preferred_element_type=jnp.float32
    )
    product = product.reshape(sources, items, rows, columns)
    returned = lax.all_to_all(product, "pair", split_axis=0, concat_axis=0, tiled=True)
    mine = returned[target, place]
    selector = (tile_occ[None, :] == jnp.arange(OBLK, dtype=jnp.int32)[:, None]).astype(jnp.float32)
    local = jnp.einsum("bs,src->brc", selector, mine, precision=lax.Precision.HIGHEST)
    return lax.psum_scatter(local, "red", scatter_dimension=2, tiled=True)


def solution(mesh):
    return jax.shard_map(
        shards,
        mesh=mesh,
        in_specs=(P("pair", None, "red"), P("pair"), P("pair", None), P(), P("pair", "red", None)),
        out_specs=P("pair", None, "red"),
        check_vma=False,
    )
```

profile of v0, /device:TPU:1, one launch (start us, length us, event | category | flops | bytes accessed | tf_op | source)
XLA Modules:
  0.0 317.5 jit_solution(16266434126403609293)
XLA Ops:
  6.5 0.0 copy-start
  6.5 0.0 reduce-scatter.4.cloned.1.call-start
  6.5 0.7 fusion.9
  7.2 0.0 copy-done
  7.2 0.7 gather_fusion
  7.9 0.2 convert_reduce_fusion
  8.1 4.8 %broadcast_in_dim.2 = f32[32,2,16,2304]{3,2,1,0:T(8,128)} broadcast(f32[]{:T(128)} %constant.4.clone.1), dimensions={} | broadcast | bytes 9437188 | tf_op jit(solution)/shard_map/broadcast_in_dim | solution.py:19
  12.9 9.2 %scatter_fusion = f32[32,2,16,2304]{3,2,1,0:T(8,128)} fusion(f32[32,2,16,2304]{3,2,1,0:T(8,128)} %broadcast_in_dim.2, s32[32]{0:T(128)S(1)} %get-tuple-element.6, f32[32,16,2304]{2,1,0:T(8,128)} %param.5), kind=kCustom, calls=%fused_computation.2 | custom fusion | bytes 14156032 | tf_op jit(solution)/shard_map/scatter | solution.py:19
  22.1 115.4 %all_to_all.10 = f32[32,2,16,2304]{3,2,1,0:T(8,128)S(1)} all-to-all(f32[32,2,16,2304]{3,2,1,0:T(8,128)} %scatter_fusion), channel_id=1, replica_groups=mesh['pair'=32,'red'=4] {'pair'}, dimensions={0} | all-to-all | bytes 18874368 | tf_op jit(solution)/shard_map/all_to_all | solution.py:20
  137.4 46.9 %fusion = f32[32,2,16,1536]{3,2,1,0:T(8,128)S(1)} fusion(f32[32,2,16,2304]{3,2,1,0:T(8,128)S(1)} %all_to_all.10, f32[1,2304,1536]{2,1,0:T(8,128)} %param.9), kind=kOutput, calls=%fused_computation.3 | convolution fusion | flops 43486543872 | bytes 29884416 | tf_op jit(solution)/shard_map/dot_general | solution.py:24
  184.4 76.9 %all_to_all.11 = f32[32,2,16,1536]{3,2,1,0:T(8,128)} all-to-all(f32[32,2,16,1536]{3,2,1,0:T(8,128)S(1)} %fusion), channel_id=1, replica_groups=mesh['pair'=32,'red'=4] {'pair'}, dimensions={0} | all-to-all | bytes 12582912 | tf_op jit(solution)/shard_map/all_to_all | solution.py:28
  261.3 0.0 copy-start.2
  261.3 3.5 %gather_fusion.1 = f32[32,16,1536]{2,1,0:T(8,128)S(1)} fusion(f32[32,2,16,1536]{3,2,1,0:T(8,128)} %all_to_all.11, s32[32]{0:T(128)S(1)} %get-tuple-element.5), kind=kCustom, calls=%fused_computation.1 | custom fusion | bytes 6291712 | tf_op jit(solution)/shard_map/gather | solution.py:29
  264.9 0.0 copy-done.2
  264.9 2.9 fusion.2
  267.8 8.2 %copy.14 = f32[4,16,1536]{0,1,2:T(8,128)} copy(f32[4,16,1536]{2,0,1:T(4,128)S(1)} %fusion.2) | data formatting | bytes 786432
  276.0 0.0 copy-start.1
  276.0 9.9 %reshape.55 = f32[1536,64]{1,0:T(8,128)} reshape(f32[1536,16,4]{2,1,0:T(8,128)} %bitcast.41) | data formatting | bytes 786432
  285.9 0.0 reduce-scatter.4.cloned.1.call-update
  285.9 20.3 %reduce-scatter.4.cloned.1.call-done = f32[384,64]{1,0:T(8,128)} async-done(((f32[1536,64]{1,0:T(8,128)}), f32[384,64]{1,0:T(8,128)}) %reduce-scatter.4.cloned.1.call-update) | async-done | bytes 98320
  306.2 2.6 reshape.56
  308.8 1.8 copy.12
  310.7 0.0 copy-done.1
  (2 shorter events, 0.0 us)
Async XLA Ops:
  6.5 0.7 copy-start
  6.5 299.7 %reduce-scatter.4.cloned.1.call-start = ((), (), s32[]{:S(2)}) async-start(), calls=%async_computation.3 | async-start | bytes 983040
  261.3 3.6 %copy-start.2 = (s32[32]{0:T(128)S(1)}, s32[32]{0:T(128)}, u32[]{:S(2)}) copy-start(s32[32]{0:T(128)} %param.6) | copy-start | bytes 388
  276.0 34.7 %copy-start.1 = (s32[32]{0:T(128)S(1)}, s32[32]{0:T(128)}, u32[]{:S(2)}) copy-start(s32[32]{0:T(128)} %param.8) | copy-start | bytes 388
Sparse Core Ops, SparseCore 0:
  286.0 20.1 reduce-scatter.3
where the time goes:
time: 318 us
  blocking collectives  192 us (60%)
  matrix products  49.8 us (16%)
  local copies, waits for them, and re-layouts  40.7 us (13%)
  waiting for transfers between devices  20.3 us (6%)
  between operations  13.4 us (4%)
    all_to_all x1, blocking collectives, shards(): lax.all_to_all(outgoing, 'pair', split_axis=0, concat_axis=0, tiled=True)  115 us
    all_to_all x1, blocking collectives, shards(): lax.all_to_all(product, 'pair', split_axis=0, concat_axis=0, tiled=True)  76.9 us
    dot_general x1, matrix products, shards(): jnp.dot(flat, block, precision=lax.Precision.HIGHEST, preferred_element_t...  46.9 us
    unnamed x9, local copies, waits for them, and re-layouts  20.7 us
    unnamed x2, waiting for transfers between devices  20.3 us
    scatter x1, local copies, waits for them, and re-layouts, shards(): jnp.zeros((peers, CAP, rows, inner), jnp.float32).at[target, place]  9.15 us
  transfers between devices with their start and end apart: 1, of which 1 were waited for; matrix products, arithmetic and copies ran while one was open for 0% of the time, Pallas kernels for 0%

commit v1 on v0

v1 whole, which is shorter than its diff:
```python
import functools

import jax
import jax.numpy as jnp
from jax import lax
from jax.experimental import pallas as pl
from jax.experimental.pallas import tpu as pltpu
from jax.sharding import PartitionSpec as P

MESH = pl.DeviceIdType.MESH
OBLK = 4
ROWS = 16
KDIM = 2304
NCOL = 1536
ZCOL = 384
NONE = 1 << 20

OFFSETS = (
    (0, 0), (1, 0),
    (0, 1), (3, 0),
    (0, 3), (1, 1),
    (3, 3), (1, 3),
    (3, 1), (2, 0),
    (0, 2), (2, 2),
    (2, 1), (2, 3),
    (1, 2), (3, 2),
)
GROUPS = 8
RELAYED = 12
RELAY_VIA = ((2, 0), (2, 0), (0, 2), (0, 2))
RELAY_ON = ((0, 1), (0, 3), (1, 0), (3, 0))
WINDOW = 3


def kernel(code0, code1, holds, amp_hbm, int_hbm, out_ref,
           amp, packed, relay, got, bhi, blo, stage, lhs, prod, zgot, summed, back,
           amp_sem, stage_sem, send_sem, got_sem, relay_send, relay_sem, forward_send,
           z_send, z_sem, back_send, back_sem):
    me = lax.axis_index("pair")
    z = lax.axis_index("red")
    x, y, c = me // 8, (me // 2) % 4, me % 2

    def chip(off, sign=1):
        dx, dy = off
        if sign < 0:
            dx, dy = 4 - dx, 4 - dy
        return lax.rem(x + dx, 4) * 4 + lax.rem(y + dy, 4)

    def remote(src, dst, ssem, rsem, pair, layer):
        return pltpu.make_async_remote_copy(
            src_ref=src, dst_ref=dst, send_sem=ssem, recv_sem=rsem,
            device_id=(pair, layer), device_id_type=MESH)

    barrier = pltpu.get_barrier_semaphore()

    def greet(i, carry):
        pl.semaphore_signal(barrier, inc=1, device_id=(lax.rem(me + i, 32), z), device_id_type=MESH)
        return carry

    lax.fori_loop(1, 32, greet, 0)
    for i in range(1, 4):
        pl.semaphore_signal(barrier, inc=1, device_id=(me, lax.rem(z + i, 4)), device_id_type=MESH)

    amp_copy = pltpu.make_async_copy(amp_hbm, amp, amp_sem)
    amp_copy.start()

    def load_stage(i):
        return pltpu.make_async_copy(int_hbm.at[0, pl.ds(i * 256, 256), :], stage.at[i % 2], stage_sem.at[i % 2])

    load_stage(0).start()
    load_stage(1).start()
    amp_copy.wait()

    def codes(k, oc):
        v = holds[chip(OFFSETS[k]) * 2 + oc]
        return code0[v], code1[v]

    def pack(k):
        for oc in range(2):
            first, second = codes(k, oc)
            one = jnp.where(first < NONE, first, 0) // OBLK
            two = jnp.where(second > first, second, 0) // OBLK
            packed[k, oc, 0:ROWS, :] = amp[one]
            packed[k, oc, ROWS:2 * ROWS, :] = amp[two]

    def send(k):
        if k >= RELAYED:
            r = k - RELAYED
            remote(packed.at[k], relay.at[r], relay_send.at[r], relay_sem.at[r],
                   chip(RELAY_VIA[r]) * 2 + c, z).start()
        elif k == 0:
            remote(packed.at[0, 1 - c], got.at[0, c], send_sem.at[0, 0], got_sem.at[0, c], me + 1 - 2 * c, z).start()
            pltpu.make_async_copy(packed.at[0, c], got.at[0, c], got_sem.at[0, c]).start()
        else:
            for oc in range(2):
                remote(packed.at[k, oc], got.at[k, c], send_sem.at[k, oc], got_sem.at[k, c],
                       chip(OFFSETS[k]) * 2 + oc, z).start()

    def forward(r):
        remote(packed.at[0], relay.at[r], relay_send.at[r], relay_sem.at[r], me + 1 - 2 * c, z).wait_recv()
        for oc in range(2):
            remote(relay.at[r, oc], got.at[RELAYED + r, c], forward_send.at[r, oc], got_sem.at[RELAYED + r, c],
                   chip(RELAY_ON[r]) * 2 + oc, z).start()

    first = [0, 1, 2, 3, 12, 13, 14, 15, 4, 5]
    for k in first[:4]:
        pack(k)
    pl.semaphore_wait(barrier, 34)
    for k in first[:4]:
        send(k)
    for k in first[4:]:
        pack(k)
        send(k)

    def split(i):
        load_stage(i).wait()
        block = stage.at[i % 2]

        def rows(t, carry):
            at = pl.multiple_of(t * 16, 16)
            for q in range(4):
                part = block[pl.ds(at, 16), q * ZCOL:(q + 1) * ZCOL]
                high = part.astype(jnp.bfloat16)
                to = pl.ds(pl.multiple_of(i * 256 + at, 16), 16)
                bhi[q, to, :] = high
                blo[q, to, :] = (part - high.astype(jnp.float32)).astype(jnp.bfloat16)
            return carry

        lax.fori_loop(0, 16, rows, 0)

    for i in range(9):
        split(i)
        if i + 2 < 9:
            load_stage(i + 2).start()

    def give_back(j):
        for i in range(3):
            remote(prod.at[j, i], zgot.at[j, i], z_send.at[j, i], z_sem.at[j, i], me, lax.rem(z + 1, 4)).wait_recv()

        def rows(t, carry):
            at = pl.ds(pl.multiple_of(t * 16, 16), 16)
            summed[j, at, :] = (prod[j, 3, at, :] + zgot[j, 0, at, :]) + (zgot[j, 1, at, :] + zgot[j, 2, at, :])
            return carry

        lax.fori_loop(0, 8, rows, 0)

    def send_back(j):
        for k in (2 * j, 2 * j + 1):
            for cs in range(2):
                part = summed.at[j, pl.ds((k - 2 * j) * 64 + cs * 32, 32), :]
                if k == 0:
                    continue
                remote(part, back.at[k, c], back_send.at[k, cs], back_sem.at[k, c],
                       chip(OFFSETS[k], -1) * 2 + cs, z).start()
            if k == 0:
                other = summed.at[0, pl.ds((1 - c) * 32, 32), :]
                remote(other, back.at[0, c], back_send.at[0, 0], back_sem.at[0, c], me + 1 - 2 * c, z).start()
                mine = summed.at[0, pl.ds(c * 32, 32), :]
                pltpu.make_async_copy(mine, back.at[0, c], back_sem.at[0, c]).start()

    def group(j, carry):
        for jj in range(GROUPS):
            @pl.when(j == jj)
            def _():
                if jj + WINDOW < 6:
                    for k in (2 * (jj + WINDOW), 2 * (jj + WINDOW) + 1):
                        pack(k)
                        send(k)
                if jj == 3:
                    forward(0)
                    forward(1)
                if jj == 4:
                    forward(2)
                    forward(3)

        for t in range(2):
            for cs in range(2):
                k = 2 * j + t
                remote(packed.at[0, 0], got.at[k, cs], send_sem.at[0, 0], got_sem.at[k, cs],
                       me + 1 - 2 * c, z).wait_recv()

        def rows(t, carry):
            k, at = 2 * j + t // 4, pl.ds(pl.multiple_of((t % 2) * 16, 16), 16)
            part = got[k, (t // 2) % 2, at, :]
            high = part.astype(jnp.bfloat16)
            to = pl.multiple_of(t * 16, 16)
            lhs[pl.ds(to, 16), :] = high
            lhs[pl.ds(to + 128, 16), :] = (part - high.astype(jnp.float32)).astype(jnp.bfloat16)
            return carry

        lax.fori_loop(0, 8, rows, 0)

        def columns(i, carry):
            layer = lax.rem(z + 1 + i, 4)
            both = jnp.dot(lhs[...], bhi[layer], preferred_element_type=jnp.float32)
            low = jnp.dot(lhs[0:128, :], blo[layer], preferred_element_type=jnp.float32)
            prod[j, i] = both[0:128] + (both[128:256] + low)

            @pl.when(i < 3)
            def _():
                remote(prod.at[j, i], zgot.at[j, i], z_send.at[j, i], z_sem.at[j, i], me, layer).start()

            return carry

        lax.fori_loop(0, 4, columns, 0)

        @pl.when(j > 0)
        def _():
            give_back(j - 1)

        for jj in range(1, GROUPS):
            @pl.when(j == jj)
            def _():
                send_back(jj - 1)

        return carry

    lax.fori_loop(0, GROUPS, group, 0)
    give_back(GROUPS - 1)
    send_back(GROUPS - 1)

    out_ref[...] = jnp.zeros_like(out_ref)
    for k in range(16):
        for oc in range(2):
            remote(summed.at[0, pl.ds(0, 32), :], back.at[k, oc], back_send.at[0, 0], back_sem.at[k, oc],
                   me + 1 - 2 * c, z).wait_recv()
        for oc in range(2):
            one, two = codes(k, oc)
            used = (one < NONE, two > one)
            for s, code in enumerate((one, two)):
                term = back[k, oc, s * ROWS:(s + 1) * ROWS, :]
                for b in range(OBLK):
                    weight = jnp.where(used[s] & (code % OBLK == b), 1.0, 0.0)
                    out_ref[b] += weight * term

    for k in range(16):
        if k >= RELAYED:
            r = k - RELAYED
            remote(packed.at[k], relay.at[r], relay_send.at[r], relay_sem.at[r], me + 1 - 2 * c, z).wait_send()
            for oc in range(2):
                remote(relay.at[r, oc], got.at[k, c], forward_send.at[r, oc], got_sem.at[k, c],
                       me + 1 - 2 * c, z).wait_send()
        else:
            for oc in range(1 if k == 0 else 2):
                remote(packed.at[k, oc], got.at[k, c], send_sem.at[k, oc], got_sem.at[k, c],
                       me + 1 - 2 * c, z).wait_send()
        for cs in range(1 if k == 0 else 2):
            remote(summed.at[0, pl.ds(0, 32), :], back.at[k, c], back_send.at[k, cs], back_sem.at[k, c],
                   me + 1 - 2 * c, z).wait_send()

    def drain(j, carry):
        for i in range(3):
            remote(prod.at[j, i], zgot.at[j, i], z_send.at[j, i], z_sem.at[j, i], me, lax.rem(z + 1, 4)).wait_send()
        return carry

    lax.fori_loop(0, GROUPS, drain, 0)


def shards(amplitudes, tile_occ, tile_virt, owner, integrals):
    slots = amplitudes.shape[0]
    ids = jnp.arange(32, dtype=jnp.int32)
    code = jnp.arange(slots, dtype=jnp.int32) * OBLK + tile_occ
    names = tile_virt[:, 0][:, None] == ids[None, :]
    code0 = jnp.min(jnp.where(names, code[:, None], NONE), axis=0)
    code1 = jnp.max(jnp.where(names, code[:, None], -1), axis=0)
    holds = jnp.sum(jnp.where(owner[:, None] == ids[None, :], ids[:, None], 0), axis=0)
    f32, bf16 = jnp.float32, jnp.bfloat16
    dma = pltpu.SemaphoreType.DMA
    return pl.pallas_call(
        kernel,
        out_shape=jax.ShapeDtypeStruct((OBLK, ROWS, ZCOL), f32),
        in_specs=[pl.BlockSpec(memory_space=pltpu.SMEM)] * 3 + [pl.BlockSpec(memory_space=pl.ANY)] * 2,
        out_specs=pl.BlockSpec(memory_space=pltpu.VMEM),
        scratch_shapes=[
            pltpu.VMEM((slots, ROWS, KDIM), f32),
            pltpu.VMEM((16, 2, 2 * ROWS, KDIM), f32),
            pltpu.VMEM((4, 2, 2 * ROWS, KDIM), f32),
            pltpu.VMEM((16, 2, 2 * ROWS, KDIM), f32),
            pltpu.VMEM((4, KDIM, ZCOL), bf16),
            pltpu.VMEM((4, KDIM, ZCOL), bf16),
            pltpu.VMEM((2, 256, NCOL), f32),
            pltpu.VMEM((256, KDIM), bf16),
            pltpu.VMEM((GROUPS, 4, 128, ZCOL), f32),
            pltpu.VMEM((GROUPS, 3, 128, ZCOL), f32),
            pltpu.VMEM((GROUPS, 128, ZCOL), f32),
            pltpu.VMEM((16, 2, 2 * ROWS, ZCOL), f32),
            dma, dma((2,)), dma((16, 2)), dma((16, 2)), dma((4,)), dma((4,)), dma((4, 2)),
            dma((GROUPS, 3)), dma((GROUPS, 3)), dma((16, 2)), dma((16, 2)),
        ],
        compiler_params=pltpu.CompilerParams(
            collective_id=0, has_side_effects=True, vmem_limit_bytes=64 * 2**20 - 2**17),
        cost_estimate=pl.CostEstimate(
            flops=6 * 1024 * KDIM * NCOL, bytes_accessed=4 * (KDIM * NCOL + slots * ROWS * KDIM), transcendentals=0),
    )(code0, code1, holds, amplitudes, integrals)


def solution(mesh):
    return jax.shard_map(
        shards,
        mesh=mesh,
        in_specs=(P("pair", None, "red"), P("pair"), P("pair", None), P(), P("pair", "red", None)),
        out_specs=P("pair", None, "red"),
        check_vma=False,
    )
```

time: 318 us -> 146 us (0.46)
  blocking collectives: 192 us -> 0 us
  Pallas kernels: 0 us -> 142 us
  matrix products: 49.8 us -> 0 us
  local copies, waits for them, and re-layouts: 40.7 us -> 1.54 us
  waiting for transfers between devices: 20.3 us -> 0 us
  between operations: 13.4 us -> 0.01 us
    all_to_all x2 -> x0, blocking collectives: 192 us -> none  [the longest x1 115 us: shards(): lax.all_to_all(outgoing, 'pair', split_axis=0, concat_axis=0, tiled=True)]
    pallas_call x0 -> x1, Pallas kernels: none -> 142 us  [shards(): pl.pallas_call(kernel, out_shape=jax.ShapeDtypeStruct((OBLK, ROWS, ZCOL),...]
    dot_general x2 -> x0, matrix products: 49.8 us -> none  [the longest x1 46.9 us: shards(): jnp.dot(flat, block, precision=lax.Precision.HIGHEST, preferred_element_t...]
    unnamed x2 -> x0, waiting for transfers between devices: 20.3 us -> none
    unnamed x9 -> x1, local copies, waits for them, and re-layouts: 20.7 us -> 1.54 us
    scatter x1 -> x0, local copies, waits for them, and re-layouts: 9.15 us -> none  [shards(): jnp.zeros((peers, CAP, rows, inner), jnp.float32).at[target, place]]
    broadcast_in_dim x1 -> x0, local copies, waits for them, and re-layouts: 4.79 us -> none  [shards(): jnp.zeros((peers, CAP, rows, inner), jnp.float32).at[target, place]]
    gather x2 -> x0, local copies, waits for them, and re-layouts: 4.25 us -> none  [the longest x1 3.55 us: shards(): mine = returned[target, place]]
  transfers between devices with their start and end apart: 1 -> 0, of which waited for: 1 -> 0; matrix products, arithmetic and copies ran while one was open for 0% -> 0% of each run, Pallas kernels for 0% -> 0%
where the time goes in v1:
time: 146 us
  Pallas kernels  142 us (97%)
  other arithmetic  2.02 us (1%)
  local copies, waits for them, and re-layouts  1.54 us (1%)
    pallas_call x1, Pallas kernels, shards(): pl.pallas_call(kernel, out_shape=jax.ShapeDtypeStruct((OBLK, ROWS, ZCOL),...  142 us

profile of v1, /device:TPU:1, one launch (start us, length us, event | category | flops | bytes accessed | tf_op | source)
XLA Modules:
  0.0 145.7 jit_solution(8908740678127950956)
XLA Ops:
  0.0 0.7 multiply_add_fusion
  0.7 1.4 select_reduce_fusion.1
  2.0 142.2 %shard_map.55 = f32[4,16,384]{2,1,0:T(8,128)} custom-call(s32[32]{0:T(128)} %get-tuple-element.6.code0, s32[32]{0:T(128)} %get-tuple-element.5.code1, s32[32]{0:T(128)} %get-tuple-element.7.holds, f32[32,16,2304]{2,1,0:T(8,128)} %amp_hbm.1, f32[1,2304,1536]{2,1,0:T(8,128)} %int_hbm.1), custom_call_target="tpu_custom_call" | custom-call | flops 21743271936 | bytes 18874368 | tf_op jit(solution)/shard_map/pallas_call | solution.py:269
  144.2 1.5 %copy.7 = f32[4,16,384]{2,1,0:T(8,128)} copy(f32[4,16,384]{2,1,0:T(8,128)} %shard_map.55) | data formatting | bytes 196608

commit v2 on v0

v2 whole, which is shorter than its diff:
```python
import functools

import jax
import jax.numpy as jnp
from jax import lax
from jax.experimental import pallas as pl
from jax.experimental.pallas import tpu as pltpu
from jax.sharding import PartitionSpec as P

MESH = pl.DeviceIdType.MESH
OBLK = 4
ROWS = 16
KDIM = 2304
NCOL = 1536
ZCOL = 384
NONE = 1 << 20

OFFSETS = (
    (0, 0), (1, 0),
    (0, 1), (3, 0),
    (0, 3), (1, 1),
    (3, 3), (1, 3),
    (3, 1), (2, 0),
    (0, 2), (2, 2),
    (2, 1), (2, 3),
    (1, 2), (3, 2),
)
GROUPS = 8
RELAYED = 12
RELAY_VIA = ((2, 0), (2, 0), (0, 2), (0, 2))
RELAY_ON = ((0, 1), (0, 3), (1, 0), (3, 0))
LATER = {0: (12, 13, 14, 15), 1: (6, 7), 2: (8, 9), 3: (10, 11)}
ON = {3: (0, 1), 4: (2, 3)}


def split_rows(block, bhi, blo, start, z):
    def rows(t, carry):
        at = pl.multiple_of(t * 16, 16)
        to = pl.ds(pl.multiple_of(start + at, 16), 16)
        for q in range(4):
            part = block[pl.ds(at, 16), q * ZCOL:(q + 1) * ZCOL]
            high = part.astype(jnp.bfloat16)
            slot = lax.rem(q + 3 - z, 4) if q else 3 - z
            half, cols = slot // 2, pl.ds(pl.multiple_of(slot % 2 * ZCOL, 128), ZCOL)
            bhi[half, to, cols] = high
            blo[half, to, cols] = (part - high.astype(jnp.float32)).astype(jnp.bfloat16)
        return carry

    lax.fori_loop(0, 16, rows, 0)


def kernel(code0, code1, holds, amp_hbm, int_hbm, out_ref, spill_ref,
           amp, packed, relay, got, bhi, blo, stage, lhs, prod, zgot, summed, back, over, under, notes, noted,
           amp_sem, stage_sem, send_sem, got_sem, relay_send, relay_sem, forward_send, cross_send,
           z_send, z_sem, back_send, back_sem, over_send, over_sem, note_send, note_sem):
    me = lax.axis_index("pair")
    z = lax.axis_index("red")
    x, y, c = me // 8, (me // 2) % 4, me % 2
    twin = me + 1 - 2 * c

    def device(off, core, sign=1):
        dx, dy = off
        if sign < 0:
            dx, dy = 4 - dx, 4 - dy
        return (lax.rem(x + dx, 4) * 4 + lax.rem(y + dy, 4)) * 2 + core

    def remote(src, dst, ssem, rsem, pair, layer):
        return pltpu.make_async_remote_copy(
            src_ref=src, dst_ref=dst, send_sem=ssem, recv_sem=rsem,
            device_id=(pair, layer), device_id_type=MESH)

    def received(dst, rsem):
        remote(dst, dst, send_sem.at[0, 0], rsem, twin, z).wait_recv()

    def sent(src, ssem):
        remote(src, src, ssem, got_sem.at[0, 0], twin, z).wait_send()

    barrier = pltpu.get_barrier_semaphore()

    def greet(i, carry):
        pl.semaphore_signal(barrier, inc=1, device_id=(lax.rem(me + i, 32), z), device_id_type=MESH)
        return carry

    lax.fori_loop(1, 32, greet, 0)
    for i in range(1, 4):
        pl.semaphore_signal(barrier, inc=1, device_id=(me, lax.rem(z + i, 4)), device_id_type=MESH)

    amp_copy = pltpu.make_async_copy(amp_hbm, amp, amp_sem)
    amp_copy.start()

    def load_stage(i):
        return pltpu.make_async_copy(int_hbm.at[0, pl.ds(i * 256, 256), :], stage.at[i % 2], stage_sem.at[i % 2])

    load_stage(0).start()
    load_stage(1).start()
    amp_copy.wait()

    def codes(k):
        near, far = holds[device(OFFSETS[k], c)], holds[device(OFFSETS[k], 1 - c)]
        return code0[near], code1[near], code0[far], code1[far]

    def pack(k):
        near0, near1, far0, far1 = codes(k)
        second = jnp.where(near1 > near0, near1, jnp.where(far1 > far0, far1, 0))
        packed[k, 0] = amp[jnp.where(far0 < NONE, far0, 0) // OBLK]
        packed[k, 1] = amp[jnp.where(near0 < NONE, near0, 0) // OBLK]
        packed[k, 2] = amp[second // OBLK]

    def send(k):
        if k >= RELAYED:
            r = k - RELAYED
            remote(packed.at[k], relay.at[r], relay_send.at[r], relay_sem.at[r], device(RELAY_VIA[r], c), z).start()
            return
        remote(packed.at[k, 0], got.at[k, 1, 0], send_sem.at[k, 0], got_sem.at[k, 1],
               device(OFFSETS[k], 1 - c), z).start()
        if k == 0:
            pltpu.make_async_copy(packed.at[0, pl.ds(1, 2)], got.at[0, 0], got_sem.at[0, 0]).start()
        else:
            remote(packed.at[k, pl.ds(1, 2)], got.at[k, 0], send_sem.at[k, 1], got_sem.at[k, 0],
                   device(OFFSETS[k], c), z).start()

    def forward(r):
        received(relay.at[r], relay_sem.at[r])
        k = RELAYED + r
        remote(relay.at[r, 0], got.at[k, 1, 0], forward_send.at[r, 0], got_sem.at[k, 1],
               device(RELAY_ON[r], 1 - c), z).start()
        remote(relay.at[r, pl.ds(1, 2)], got.at[k, 0], forward_send.at[r, 1], got_sem.at[k, 0],
               device(RELAY_ON[r], c), z).start()

    for k in range(4):
        pack(k)
    left = jnp.int32(0)
    for k in range(16):
        near0, near1, far0, far1 = codes(k)
        left = left + jnp.where((near1 > near0) & (far1 > far0), 1, 0)
    top = lax.broadcasted_iota(jnp.int32, (8, 128), 0) < 4
    for k in range(16):
        near0, near1, far0, far1 = codes(k)
        mine = jnp.where(near1 > near0, 1.0, 0.0)
        notes[2 * k] = jnp.where(top, mine, left.astype(jnp.float32))
        notes[2 * k + 1] = jnp.where(top, 1.0 - mine, left.astype(jnp.float32))
    pl.semaphore_wait(barrier, 34)
    for k in range(16):
        remote(notes.at[2 * k + 1], noted.at[2 * k + 1], note_send, note_sem, device(OFFSETS[k], 1 - c), z).start()
        if k == 0:
            noted[0] = notes[0]
        else:
            remote(notes.at[2 * k], noted.at[2 * k], note_send, note_sem, device(OFFSETS[k], c), z).start()
    for k in range(4):
        send(k)
    for k in range(4, 6):
        pack(k)
        send(k)

    for i in range(9):
        load_stage(i).wait()
        split_rows(stage.at[i % 2], bhi, blo, i * 256, z)
        if i + 2 < 9:
            load_stage(i + 2).start()

    received(noted.at[pl.ds(1, 31)], note_sem)

    def share_group(j):
        received(under.at[j], over_sem.at[j])
        for n in range(4):
            prod[j, n, 64:96, :] += under[j, :, n * ZCOL:(n + 1) * ZCOL]
            if n < 3:
                remote(prod.at[j, n], zgot.at[j, n], z_send.at[j, n], z_sem.at[j, n], me, lax.rem(z + 1 + n, 4)).start()

    def reduce_group(j):
        for i in range(3):
            received(zgot.at[j, i], z_sem.at[j, i])
        for role in range(3):
            for t in range(2):
                at = slice(role * 32 + t * 16, role * 32 + t * 16 + 16)
                summed[j, t, (0, 2, 1)[role]] = (prod[j, 3, at, :] + zgot[j, 0, at, :]) + (zgot[j, 1, at, :] + zgot[j, 2, at, :])

    def send_back(j):
        for t in range(2):
            k = 2 * j + t
            near, far = summed.at[j, t, pl.ds(0, 2)], summed.at[j, t, 2]
            remote(far, back.at[k, 2], back_send.at[k, 1], back_sem.at[k, 1], device(OFFSETS[k], 1 - c, -1), z).start()
            if k == 0:
                pltpu.make_async_copy(near, back.at[0, pl.ds(0, 2)], back_sem.at[0, 0]).start()
            else:
                remote(near, back.at[k, pl.ds(0, 2)], back_send.at[k, 0], back_sem.at[k, 0],
                       device(OFFSETS[k], c, -1), z).start()

    def group(j, carry):
        for jj in range(GROUPS):
            @pl.when(j == jj)
            def _():
                for k in LATER.get(jj, ()):
                    pack(k)
                    send(k)
                for r in ON.get(jj, ()):
                    forward(r)

        for t in range(2):
            k = 2 * j + t
            received(got.at[k, 0], got_sem.at[k, 0])
            remote(got.at[k, 0, 1], got.at[k, 1, 1], cross_send.at[k], got_sem.at[k, 2], twin, z).start()
        for t in range(2):
            k = 2 * j + t
            received(got.at[k, 1, 0], got_sem.at[k, 1])
            received(got.at[k, 1, 1], got_sem.at[k, 2])

        def place(t, part):
            high = part.astype(jnp.bfloat16)
            to = pl.multiple_of(t * 16, 16)
            lhs[pl.ds(to, 16), :] = high
            lhs[pl.ds(to + 128, 16), :] = (part - high.astype(jnp.float32)).astype(jnp.bfloat16)

        def first_tiles(t, carry):
            place(t, got[2 * j + t % 2, t // 2, 0])
            return carry

        def second_tiles(t, carry):
            k, side = 2 * j + t % 2, t // 2
            place(t + 4, got[k, side, 1] * noted[2 * k + side, 0:1, 0:1])
            return carry

        lax.fori_loop(0, 4, first_tiles, 0)
        lax.fori_loop(0, 4, second_tiles, 0)

        @pl.when(j > 0)
        def _():
            share_group(j - 1)

        def columns(i, carry):
            both = jnp.dot(lhs[...], bhi[i], preferred_element_type=jnp.float32)
            low = jnp.dot(lhs[0:128, :], blo[i], preferred_element_type=jnp.float32)
            term = both[0:128] + (both[128:256] + low)
            prod[j, 2 * i] = term[0:96, 0:ZCOL]
            prod[j, 2 * i + 1] = term[0:96, ZCOL:2 * ZCOL]
            over[j, :, pl.ds(pl.multiple_of(i * 2 * ZCOL, 128), 2 * ZCOL)] = term[96:128]
            return carry

        lax.fori_loop(0, 2, columns, 0)
        remote(over.at[j], under.at[j], over_send.at[j], over_sem.at[j], twin, z).start()

        @pl.when(j > 1)
        def _():
            reduce_group(j - 2)

        for jj in range(2, GROUPS):
            @pl.when(j == jj)
            def _():
                send_back(jj - 2)

        return carry

    lax.fori_loop(0, GROUPS, group, 0)
    share_group(GROUPS - 1)
    for j in (GROUPS - 2, GROUPS - 1):
        reduce_group(j)
        send_back(j)

    out_ref[...] = jnp.zeros_like(out_ref)
    for k in range(16):
        near0, near1, far0, far1 = codes(k)
        second = jnp.where(near1 > near0, near1, far1)
        tiles = ((near0, near0 < NONE), (second, (near1 > near0) | (far1 > far0)), (far0, far0 < NONE))
        received(back.at[k, pl.ds(0, 2)], back_sem.at[k, 0])
        received(back.at[k, 2], back_sem.at[k, 1])
        for s, (code, used) in enumerate(tiles):
            term = back[k, s]
            for b in range(OBLK):
                weight = jnp.where(used & (code % OBLK == b), 1.0, 0.0)
                out_ref[b] += weight * term

    spill = noted[0]
    for i in range(1, 32):
        spill = jnp.maximum(spill, noted[i])
    spill_ref[...] = spill

    for k in range(16):
        if k >= RELAYED:
            r = k - RELAYED
            sent(packed.at[k], relay_send.at[r])
            sent(relay.at[r, 0], forward_send.at[r, 0])
            sent(relay.at[r, pl.ds(1, 2)], forward_send.at[r, 1])
        else:
            sent(packed.at[k, 0], send_sem.at[k, 0])
            if k > 0:
                sent(packed.at[k, pl.ds(1, 2)], send_sem.at[k, 1])
        sent(got.at[k, 0, 1], cross_send.at[k])
        sent(back.at[k, 2], back_send.at[k, 1])
        if k > 0:
            sent(back.at[k, pl.ds(0, 2)], back_send.at[k, 0])

    def drain(j, carry):
        for i in range(3):
            sent(prod.at[j, i], z_send.at[j, i])
        sent(over.at[j], over_send.at[j])
        return carry

    lax.fori_loop(0, GROUPS, drain, 0)
    sent(notes.at[pl.ds(1, 31)], note_send)


def spill_kernel(code0, code1, holds, amp_hbm, int_hbm, start_ref, out_ref,
                 amp, packed, got, bhi, blo, stage, lhs, prod, zgot, summed, back,
                 amp_sem, stage_sem, send_sem, got_sem, z_send, z_sem, back_send, back_sem):
    me = lax.axis_index("pair")
    z = lax.axis_index("red")
    x, y, c = me // 8, (me // 2) % 4, me % 2

    def device(off, core, sign=1):
        dx, dy = off
        if sign < 0:
            dx, dy = 4 - dx, 4 - dy
        return (lax.rem(x + dx, 4) * 4 + lax.rem(y + dy, 4)) * 2 + core

    def remote(src, dst, ssem, rsem, pair, layer):
        return pltpu.make_async_remote_copy(
            src_ref=src, dst_ref=dst, send_sem=ssem, recv_sem=rsem,
            device_id=(pair, layer), device_id_type=MESH)

    def received(dst, rsem):
        remote(dst, dst, send_sem.at[0], rsem, me + 1 - 2 * c, z).wait_recv()

    def sent(src, ssem):
        remote(src, src, ssem, got_sem.at[0], me + 1 - 2 * c, z).wait_send()

    barrier = pltpu.get_barrier_semaphore()

    def greet(i, carry):
        pl.semaphore_signal(barrier, inc=1, device_id=(2 * i + 1 - c, z), device_id_type=MESH)
        return carry

    lax.fori_loop(0, 16, greet, 0)
    for i in range(1, 4):
        pl.semaphore_signal(barrier, inc=1, device_id=(me, lax.rem(z + i, 4)), device_id_type=MESH)

    amp_copy = pltpu.make_async_copy(amp_hbm, amp, amp_sem)
    amp_copy.start()

    def load_stage(i):
        return pltpu.make_async_copy(int_hbm.at[0, pl.ds(i * 256, 256), :], stage.at[i % 2], stage_sem.at[i % 2])

    load_stage(0).start()
    load_stage(1).start()
    amp_copy.wait()

    def spilled(k):
        near, far = holds[device(OFFSETS[k], c)], holds[device(OFFSETS[k], 1 - c)]
        return code1[far], (code1[near] > code0[near]) & (code1[far] > code0[far])

    for k in range(16):
        code, used = spilled(k)
        packed[k] = amp[jnp.where(used, code, 0) // OBLK]
    pl.semaphore_wait(barrier, 19)
    for k in range(16):
        remote(packed.at[k], got.at[k], send_sem.at[k], got_sem.at[k], device(OFFSETS[k], 1 - c), z).start()

    for i in range(9):
        load_stage(i).wait()
        split_rows(stage.at[i % 2], bhi, blo, i * 256, z)
        if i + 2 < 9:
            load_stage(i + 2).start()

    for j in range(2):
        for k in range(8 * j, 8 * j + 8):
            received(got.at[k], got_sem.at[k])

        def rows(t, carry):
            part = got[8 * j + t]
            high = part.astype(jnp.bfloat16)
            to = pl.multiple_of(t * 16, 16)
            lhs[pl.ds(to, 16), :] = high
            lhs[pl.ds(to + 128, 16), :] = (part - high.astype(jnp.float32)).astype(jnp.bfloat16)
            return carry

        lax.fori_loop(0, 8, rows, 0)

        def columns(i, carry):
            both = jnp.dot(lhs[...], bhi[i], preferred_element_type=jnp.float32)
            low = jnp.dot(lhs[0:128, :], blo[i], preferred_element_type=jnp.float32)
            term = both[0:128] + (both[128:256] + low)
            prod[j, 2 * i] = term[:, 0:ZCOL]
            prod[j, 2 * i + 1] = term[:, ZCOL:2 * ZCOL]
            return carry

        lax.fori_loop(0, 2, columns, 0)
        for n in range(3):
            remote(prod.at[j, n], zgot.at[j, n], z_send.at[j, n], z_sem.at[j, n], me, lax.rem(z + 1 + n, 4)).start()

    for j in range(2):
        for n in range(3):
            received(zgot.at[j, n], z_sem.at[j, n])
        for t in range(8):
            k, at = 8 * j + t, slice(t * 16, t * 16 + 16)
            summed[k] = (prod[j, 3, at, :] + zgot[j, 0, at, :]) + (zgot[j, 1, at, :] + zgot[j, 2, at, :])
            remote(summed.at[k], back.at[k], back_send.at[k], back_sem.at[k], device(OFFSETS[k], 1 - c, -1), z).start()

    out_ref[...] = start_ref[...]
    for k in range(16):
        code, used = spilled(k)
        received(back.at[k], back_sem.at[k])
        for b in range(OBLK):
            weight = jnp.where(used & (code % OBLK == b), 1.0, 0.0)
            out_ref[b] += weight * back[k]

    for k in range(16):
        sent(packed.at[k], send_sem.at[k])
        sent(summed.at[k], back_send.at[k])
    for j in range(2):
        for n in range(3):
            sent(prod.at[j, n], z_send.at[j, n])


def shards(amplitudes, tile_occ, tile_virt, owner, integrals):
    slots = amplitudes.shape[0]
    ids = jnp.arange(32, dtype=jnp.int32)
    code = jnp.arange(slots, dtype=jnp.int32) * OBLK + tile_occ
    names = tile_virt[:, 0][:, None] == ids[None, :]
    code0 = jnp.min(jnp.where(names, code[:, None], NONE), axis=0)
    code1 = jnp.max(jnp.where(names, code[:, None], -1), axis=0)
    holds = jnp.sum(jnp.where(owner[:, None] == ids[None, :], ids[:, None], 0), axis=0)
    f32, bf16 = jnp.float32, jnp.bfloat16
    dma = pltpu.SemaphoreType.DMA
    out, spill = pl.pallas_call(
        kernel,
        out_shape=(jax.ShapeDtypeStruct((OBLK, ROWS, ZCOL), f32), jax.ShapeDtypeStruct((8, 128), f32)),
        in_specs=[pl.BlockSpec(memory_space=pltpu.SMEM)] * 3 + [pl.BlockSpec(memory_space=pl.ANY)] * 2,
        out_specs=(pl.BlockSpec(memory_space=pltpu.VMEM),) * 2,
        scratch_shapes=[
            pltpu.VMEM((slots, ROWS, KDIM), f32),
            pltpu.VMEM((16, 3, ROWS, KDIM), f32),
            pltpu.VMEM((4, 3, ROWS, KDIM), f32),
            pltpu.VMEM((16, 2, 2, ROWS, KDIM), f32),
            pltpu.VMEM((2, KDIM, 2 * ZCOL), bf16),
            pltpu.VMEM((2, KDIM, 2 * ZCOL), bf16),
            pltpu.VMEM((2, 256, NCOL), f32),
            pltpu.VMEM((256, KDIM), bf16),
            pltpu.VMEM((GROUPS, 4, 96, ZCOL), f32),
            pltpu.VMEM((GROUPS, 3, 96, ZCOL), f32),
            pltpu.VMEM((GROUPS, 2, 3, ROWS, ZCOL), f32),
            pltpu.VMEM((16, 3, ROWS, ZCOL), f32),
            pltpu.VMEM((GROUPS, 32, NCOL), f32),
            pltpu.VMEM((GROUPS, 32, NCOL), f32),
            pltpu.VMEM((32, 8, 128), f32),
            pltpu.VMEM((32, 8, 128), f32),
            dma, dma((2,)), dma((16, 2)), dma((16, 3)), dma((4,)), dma((4,)), dma((4, 2)), dma((16,)),
            dma((GROUPS, 3)), dma((GROUPS, 3)), dma((16, 2)), dma((16, 2)), dma((GROUPS,)), dma((GROUPS,)), dma, dma,
        ],
        compiler_params=pltpu.CompilerParams(
            collective_id=0, has_side_effects=True, vmem_limit_bytes=64 * 2**20 - 2**17),
        cost_estimate=pl.CostEstimate(
            flops=6 * 1024 * KDIM * NCOL, bytes_accessed=4 * (KDIM * NCOL + slots * ROWS * KDIM), transcendentals=0),
    )(code0, code1, holds, amplitudes, integrals)

    def add_spilled(first):
        return pl.pallas_call(
            spill_kernel,
            out_shape=jax.ShapeDtypeStruct((OBLK, ROWS, ZCOL), f32),
            in_specs=[pl.BlockSpec(memory_space=pltpu.SMEM)] * 3 + [pl.BlockSpec(memory_space=pl.ANY)] * 2
            + [pl.BlockSpec(memory_space=pltpu.VMEM)],
            out_specs=pl.BlockSpec(memory_space=pltpu.VMEM),
            scratch_shapes=[
                pltpu.VMEM((slots, ROWS, KDIM), f32),
                pltpu.VMEM((16, ROWS, KDIM), f32),
                pltpu.VMEM((16, ROWS, KDIM), f32),
                pltpu.VMEM((2, KDIM, 2 * ZCOL), bf16),
                pltpu.VMEM((2, KDIM, 2 * ZCOL), bf16),
                pltpu.VMEM((2, 256, NCOL), f32),
                pltpu.VMEM((256, KDIM), bf16),
                pltpu.VMEM((2, 4, 128, ZCOL), f32),
                pltpu.VMEM((2, 3, 128, ZCOL), f32),
                pltpu.VMEM((16, ROWS, ZCOL), f32),
                pltpu.VMEM((16, ROWS, ZCOL), f32),
                dma, dma((2,)), dma((16,)), dma((16,)), dma((2, 3)), dma((2, 3)), dma((16,)), dma((16,)),
            ],
            compiler_params=pltpu.CompilerParams(
                collective_id=1, has_side_effects=True, vmem_limit_bytes=60 * 2**20),
            cost_estimate=pl.CostEstimate(
                flops=6 * 256 * KDIM * NCOL, bytes_accessed=4 * (KDIM * NCOL + slots * ROWS * KDIM), transcendentals=0),
        )(code0, code1, holds, amplitudes, integrals, first)

    return lax.cond(spill[7, 0] > 0.0, add_spilled, lambda first: first, out)


def solution(mesh):
    return jax.shard_map(
        shards,
        mesh=mesh,
        in_specs=(P("pair", None, "red"), P("pair"), P("pair", None), P(), P("pair", "red", None)),
        out_specs=P("pair", None, "red"),
        check_vma=False,
    )
```

time: 318 us -> 127 us (0.40)
  blocking collectives: 192 us -> 0 us
  Pallas kernels: 0 us -> 122 us
  matrix products: 49.8 us -> 0 us
  local copies, waits for them, and re-layouts: 40.7 us -> 2.74 us
  waiting for transfers between devices: 20.3 us -> 0 us
  between operations: 13.4 us -> 0.68 us
    all_to_all x2 -> x0, blocking collectives: 192 us -> none  [the longest x1 115 us: shards(): lax.all_to_all(outgoing, 'pair', split_axis=0, concat_axis=0, tiled=True)]
    pallas_call x0 -> x1, Pallas kernels: none -> 122 us  [shards(): pl.pallas_call(kernel, out_shape=(jax.ShapeDtypeStruct((OBLK, ROWS, ZCOL)...]
    dot_general x2 -> x0, matrix products: 49.8 us -> none  [the longest x1 46.9 us: shards(): jnp.dot(flat, block, precision=lax.Precision.HIGHEST, preferred_element_t...]
    unnamed x2 -> x0, waiting for transfers between devices: 20.3 us -> none
    unnamed x9 -> x1, local copies, waits for them, and re-layouts: 20.7 us -> 1.54 us
    scatter x1 -> x0, local copies, waits for them, and re-layouts: 9.15 us -> none  [shards(): jnp.zeros((peers, CAP, rows, inner), jnp.float32).at[target, place]]
    broadcast_in_dim x1 -> x0, local copies, waits for them, and re-layouts: 4.79 us -> none  [shards(): jnp.zeros((peers, CAP, rows, inner), jnp.float32).at[target, place]]
    gather x2 -> x0, local copies, waits for them, and re-layouts: 4.25 us -> none  [the longest x1 3.55 us: shards(): mine = returned[target, place]]
  transfers between devices with their start and end apart: 1 -> 0, of which waited for: 1 -> 0; matrix products, arithmetic and copies ran while one was open for 0% -> 0% of each run, Pallas kernels for 0% -> 0%
where the time goes in v2:
time: 127 us
  Pallas kernels  122 us (96%)
  local copies, waits for them, and re-layouts  2.74 us (2%)
  other arithmetic  1.42 us (1%)
    pallas_call x1, Pallas kernels, shards(): pl.pallas_call(kernel, out_shape=(jax.ShapeDtypeStruct((OBLK, ROWS, ZCOL)...  122 us

profile of v2, /device:TPU:1, one launch (start us, length us, event | category | flops | bytes accessed | tf_op | source)
XLA Modules:
  0.0 127.0 jit_solution(10554294955669279518)
XLA Ops:
  0.0 0.7 multiply_add_fusion
  0.7 0.8 select_reduce_fusion.1
  1.4 122.1 %shard_map.57 = (f32[4,16,384]{2,1,0:T(8,128)}, f32[8,128]{1,0:T(8,128)}) custom-call(s32[32]{0:T(128)S(1)} %get-tuple-element.33.code0, s32[32]{0:T(128)S(1)} %get-tuple-element.32.code1, s32[32]{0:T(128)S(1)} %get-tuple-element.34.holds, f32[32,16,2304]{2,1,0:T(8,128)} %amp_hbm.1, f32[1,2304,1536]{2,1,0:T(8,128)} %int_hbm.1), custom_call_target="tpu_custom_call" | custom-call | flops 21743271936 | bytes 18874368 | tf_op jit(solution)/shard_map/pallas_call | solution.py:423
  123.6 1.2 slice.3
  125.4 1.5 %copy.13 = f32[4,16,384]{2,1,0:T(8,128)} copy(f32[4,16,384]{2,1,0:T(8,128)} %get-tuple-element.31) | data formatting | bytes 196608
  (1 shorter events, 0.0 us)

commit v3 on v2

--- a/solution.py
+++ b/solution.py
@@ -16,37 +16,39 @@
 NONE = 1 << 20
 
 OFFSETS = (
-    (0, 0), (1, 0),
-    (0, 1), (3, 0),
-    (0, 3), (1, 1),
-    (3, 3), (1, 3),
-    (3, 1), (2, 0),
-    (0, 2), (2, 2),
-    (2, 1), (2, 3),
-    (1, 2), (3, 2),
+    (0, 0), (1, 0), (0, 1), (3, 0), (0, 3),
+    (1, 1), (3, 3), (1, 3), (3, 1),
+    (2, 0), (0, 2),
+    (2, 1), (2, 3), (1, 2), (3, 2),
+    (2, 2),
 )
-GROUPS = 8
-RELAYED = 12
+STEPS = 16
+LAG = 3
+PROMPT = 13
+RELAYED, RELAYS = 11, 4
 RELAY_VIA = ((2, 0), (2, 0), (0, 2), (0, 2))
 RELAY_ON = ((0, 1), (0, 3), (1, 0), (3, 0))
-LATER = {0: (12, 13, 14, 15), 1: (6, 7), 2: (8, 9), 3: (10, 11)}
-ON = {3: (0, 1), 4: (2, 3)}
+EARLY = (0, 1, 2, 3, 4)
+MEANWHILE = {3: (5, 6), 5: (7, 8)}
+LATER = {1: (11, 12, 13, 14), 5: (9, 10), 8: (15,)}
+ON = {7: (0, 1, 2, 3)}
 
 
 def split_rows(block, bhi, blo, start, z):
     def rows(t, carry):
-        at = pl.multiple_of(t * 16, 16)
-        to = pl.ds(pl.multiple_of(start + at, 16), 16)
+        at = pl.multiple_of(t * 32, 32)
+        to = pl.ds(pl.multiple_of(start + at, 32), 32)
+        parts = [block[pl.ds(at, 32), q * ZCOL:(q + 1) * ZCOL] for q in range(4)]
+        high = [part.astype(jnp.bfloat16) for part in parts]
+        low = [(part - top.astype(jnp.float32)).astype(jnp.bfloat16) for part, top in zip(parts, high)]
         for q in range(4):
-            part = block[pl.ds(at, 16), q * ZCOL:(q + 1) * ZCOL]
-            high = part.astype(jnp.bfloat16)
             slot = lax.rem(q + 3 - z, 4) if q else 3 - z
             half, cols = slot // 2, pl.ds(pl.multiple_of(slot % 2 * ZCOL, 128), ZCOL)
-            bhi[half, to, cols] = high
-            blo[half, to, cols] = (part - high.astype(jnp.float32)).astype(jnp.bfloat16)
+            bhi[half, to, cols] = high[q]
+            blo[half, to, cols] = low[q]
         return carry
 
-    lax.fori_loop(0, 16, rows, 0)
+    lax.fori_loop(0, 8, rows, 0)
 
 
 def kernel(code0, code1, holds, amp_hbm, int_hbm, out_ref, spill_ref,
@@ -107,7 +109,7 @@
         packed[k, 2] = amp[second // OBLK]
 
     def send(k):
-        if k >= RELAYED:
+        if RELAYED <= k < RELAYED + RELAYS:
             r = k - RELAYED
             remote(packed.at[k], relay.at[r], relay_send.at[r], relay_sem.at[r], device(RELAY_VIA[r], c), z).start()
             return
@@ -127,7 +129,7 @@
         remote(relay.at[r, pl.ds(1, 2)], got.at[k, 0], forward_send.at[r, 1], got_sem.at[k, 0],
                device(RELAY_ON[r], c), z).start()
 
-    for k in range(4):
+    for k in EARLY:
         pack(k)
     left = jnp.int32(0)
     for k in range(16):
@@ -146,10 +148,7 @@
             noted[0] = notes[0]
         else:
             remote(notes.at[2 * k], noted.at[2 * k], note_send, note_sem, device(OFFSETS[k], c), z).start()
-    for k in range(4):
-        send(k)
-    for k in range(4, 6):
-        pack(k)
+    for k in EARLY:
         send(k)
 
     for i in range(9):
@@ -157,37 +156,37 @@
         split_rows(stage.at[i % 2], bhi, blo, i * 256, z)
         if i + 2 < 9:
             load_stage(i + 2).start()
+        for k in MEANWHILE.get(i, ()):
+            pack(k)
+            send(k)
 
     received(noted.at[pl.ds(1, 31)], note_sem)
 
-    def share_group(j):
+    def share(j):
         received(under.at[j], over_sem.at[j])
         for n in range(4):
-            prod[j, n, 64:96, :] += under[j, :, n * ZCOL:(n + 1) * ZCOL]
+            prod[j, n, 32:48, :] += under[j, :, n * ZCOL:(n + 1) * ZCOL]
             if n < 3:
                 remote(prod.at[j, n], zgot.at[j, n], z_send.at[j, n], z_sem.at[j, n], me, lax.rem(z + 1 + n, 4)).start()
 
-    def reduce_group(j):
+    def reduce_step(j):
         for i in range(3):
             received(zgot.at[j, i], z_sem.at[j, i])
         for role in range(3):
-            for t in range(2):
-                at = slice(role * 32 + t * 16, role * 32 + t * 16 + 16)
-                summed[j, t, (0, 2, 1)[role]] = (prod[j, 3, at, :] + zgot[j, 0, at, :]) + (zgot[j, 1, at, :] + zgot[j, 2, at, :])
-
-    def send_back(j):
-        for t in range(2):
-            k = 2 * j + t
-            near, far = summed.at[j, t, pl.ds(0, 2)], summed.at[j, t, 2]
-            remote(far, back.at[k, 2], back_send.at[k, 1], back_sem.at[k, 1], device(OFFSETS[k], 1 - c, -1), z).start()
-            if k == 0:
-                pltpu.make_async_copy(near, back.at[0, pl.ds(0, 2)], back_sem.at[0, 0]).start()
-            else:
-                remote(near, back.at[k, pl.ds(0, 2)], back_send.at[k, 0], back_sem.at[k, 0],
-                       device(OFFSETS[k], c, -1), z).start()
-
-    def group(j, carry):
-        for jj in range(GROUPS):
+            at = slice(role * 16, role * 16 + 16)
+            summed[j, (0, 2, 1)[role]] = (prod[j, 3, at, :] + zgot[j, 0, at, :]) + (zgot[j, 1, at, :] + zgot[j, 2, at, :])
+
+    def send_back(k):
+        near, far = summed.at[k, pl.ds(0, 2)], summed.at[k, 2]
+        remote(far, back.at[k, 2], back_send.at[k, 1], back_sem.at[k, 1], device(OFFSETS[k], 1 - c, -1), z).start()
+        if k == 0:
+            pltpu.make_async_copy(near, back.at[0, pl.ds(0, 2)], back_sem.at[0, 0]).start()
+        else:
+            remote(near, back.at[k, pl.ds(0, 2)], back_send.at[k, 0], back_sem.at[k, 0],
+                   device(OFFSETS[k], c, -1), z).start()
+
+    def step(j, carry):
+        for jj in range(STEPS):
             @pl.when(j == jj)
             def _():
                 for k in LATER.get(jj, ()):
@@ -196,67 +195,58 @@
                 for r in ON.get(jj, ()):
                     forward(r)
 
-        for t in range(2):
-            k = 2 * j + t
-            received(got.at[k, 0], got_sem.at[k, 0])
-            remote(got.at[k, 0, 1], got.at[k, 1, 1], cross_send.at[k], got_sem.at[k, 2], twin, z).start()
-        for t in range(2):
-            k = 2 * j + t
-            received(got.at[k, 1, 0], got_sem.at[k, 1])
-            received(got.at[k, 1, 1], got_sem.at[k, 2])
+        received(got.at[j, 0], got_sem.at[j, 0])
+        remote(got.at[j, 0, 1], got.at[j, 1, 1], cross_send.at[j], got_sem.at[j, 2], twin, z).start()
 
         def place(t, part):
             high = part.astype(jnp.bfloat16)
-            to = pl.multiple_of(t * 16, 16)
-            lhs[pl.ds(to, 16), :] = high
-            lhs[pl.ds(to + 128, 16), :] = (part - high.astype(jnp.float32)).astype(jnp.bfloat16)
-
-        def first_tiles(t, carry):
-            place(t, got[2 * j + t % 2, t // 2, 0])
-            return carry
-
-        def second_tiles(t, carry):
-            k, side = 2 * j + t % 2, t // 2
-            place(t + 4, got[k, side, 1] * noted[2 * k + side, 0:1, 0:1])
-            return carry
-
-        lax.fori_loop(0, 4, first_tiles, 0)
-        lax.fori_loop(0, 4, second_tiles, 0)
-
-        @pl.when(j > 0)
+            lhs[t * 16:t * 16 + 16, :] = high
+            lhs[t * 16 + 64:t * 16 + 80, :] = (part - high.astype(jnp.float32)).astype(jnp.bfloat16)
+
+        place(0, got[j, 0, 0])
+        place(2, got[j, 0, 1] * noted[2 * j, 0:1, 0:1])
+        received(got.at[j, 1, 0], got_sem.at[j, 1])
+        place(1, got[j, 1, 0])
+        received(got.at[j, 1, 1], got_sem.at[j, 2])
+        place(3, got[j, 1, 1] * noted[2 * j + 1, 0:1, 0:1])
+
+        @pl.when((j > 0) & (j <= PROMPT))
         def _():
-            share_group(j - 1)
+            share(j - 1)
 
         def columns(i, carry):
             both = jnp.dot(lhs[...], bhi[i], preferred_element_type=jnp.float32)
-            low = jnp.dot(lhs[0:128, :], blo[i], preferred_element_type=jnp.float32)
-            term = both[0:128] + (both[128:256] + low)
-            prod[j, 2 * i] = term[0:96, 0:ZCOL]
-            prod[j, 2 * i + 1] = term[0:96, ZCOL:2 * ZCOL]
-            over[j, :, pl.ds(pl.multiple_of(i * 2 * ZCOL, 128), 2 * ZCOL)] = term[96:128]
+            low = jnp.dot(lhs[0:64, :], blo[i], preferred_element_type=jnp.float32)
+            term = both[0:64] + (both[64:128] + low)
+            prod[j, 2 * i] = term[0:48, 0:ZCOL]
+            prod[j, 2 * i + 1] = term[0:48, ZCOL:2 * ZCOL]
+            over[j, :, pl.ds(pl.multiple_of(i * 2 * ZCOL, 128), 2 * ZCOL)] = term[48:64]
             return carry
 
         lax.fori_loop(0, 2, columns, 0)
         remote(over.at[j], under.at[j], over_send.at[j], over_sem.at[j], twin, z).start()
 
-        @pl.when(j > 1)
+        @pl.when(j >= LAG)
         def _():
-            reduce_group(j - 2)
-
-        for jj in range(2, GROUPS):
+            reduce_step(j - LAG)
+
+        for jj in range(LAG, STEPS):
             @pl.when(j == jj)
             def _():
-                send_back(jj - 2)
+                send_back(jj - LAG)
+
+        @pl.when(j >= PROMPT)
+        def _():
+            share(j)
 
         return carry
 
-    lax.fori_loop(0, GROUPS, group, 0)
-    share_group(GROUPS - 1)
-    for j in (GROUPS - 2, GROUPS - 1):
-        reduce_group(j)
+    lax.fori_loop(0, STEPS, step, 0)
+    for j in range(STEPS - LAG, STEPS):
+        reduce_step(j)
         send_back(j)
 
-    out_ref[...] = jnp.zeros_like(out_ref)
+    total = [jnp.zeros((ROWS, ZCOL), jnp.float32) for b in range(OBLK)]
     for k in range(16):
         near0, near1, far0, far1 = codes(k)
         second = jnp.where(near1 > near0, near1, far1)
@@ -267,7 +257,9 @@
             term = back[k, s]
             for b in range(OBLK):
                 weight = jnp.where(used & (code % OBLK == b), 1.0, 0.0)
-                out_ref[b] += weight * term
+                total[b] = total[b] + weight * term
+    for b in range(OBLK):
+        out_ref[b] = total[b]
 
     spill = noted[0]
     for i in range(1, 32):
@@ -275,7 +267,7 @@
     spill_ref[...] = spill
 
     for k in range(16):
-        if k >= RELAYED:
+        if RELAYED <= k < RELAYED + RELAYS:
             r = k - RELAYED
             sent(packed.at[k], relay_send.at[r])
             sent(relay.at[r, 0], forward_send.at[r, 0])
@@ -295,7 +287,7 @@
         sent(over.at[j], over_send.at[j])
         return carry
 
-    lax.fori_loop(0, GROUPS, drain, 0)
+    lax.fori_loop(0, STEPS, drain, 0)
     sent(notes.at[pl.ds(1, 31)], note_send)
 
 
@@ -360,24 +352,27 @@
         if i + 2 < 9:
             load_stage(i + 2).start()
 
-    for j in range(2):
-        for k in range(8 * j, 8 * j + 8):
+    def finish(j):
+        for n in range(3):
+            received(zgot.at[j, n], z_sem.at[j, n])
+        for t in range(4):
+            k, at = 4 * j + t, slice(t * 16, t * 16 + 16)
+            summed[k] = (prod[j, 3, at, :] + zgot[j, 0, at, :]) + (zgot[j, 1, at, :] + zgot[j, 2, at, :])
+            remote(summed.at[k], back.at[k], back_send.at[k], back_sem.at[k], device(OFFSETS[k], 1 - c, -1), z).start()
+
+    for j in range(4):
+        for t in range(4):
+            k = 4 * j + t
             received(got.at[k], got_sem.at[k])
-
-        def rows(t, carry):
-            part = got[8 * j + t]
+            part = got[k]
             high = part.astype(jnp.bfloat16)
-            to = pl.multiple_of(t * 16, 16)
-            lhs[pl.ds(to, 16), :] = high
-            lhs[pl.ds(to + 128, 16), :] = (part - high.astype(jnp.float32)).astype(jnp.bfloat16)
-            return carry
-
-        lax.fori_loop(0, 8, rows, 0)
+            lhs[t * 16:t * 16 + 16, :] = high
+            lhs[t * 16 + 64:t * 16 + 80, :] = (part - high.astype(jnp.float32)).astype(jnp.bfloat16)
 
         def columns(i, carry):
             both = jnp.dot(lhs[...], bhi[i], preferred_element_type=jnp.float32)
-            low = jnp.dot(lhs[0:128, :], blo[i], preferred_element_type=jnp.float32)
-            term = both[0:128] + (both[128:256] + low)
+            low = jnp.dot(lhs[0:64, :], blo[i], preferred_element_type=jnp.float32)
+            term = both[0:64] + (both[64:128] + low)
             prod[j, 2 * i] = term[:, 0:ZCOL]
             prod[j, 2 * i + 1] = term[:, ZCOL:2 * ZCOL]
             return carry
@@ -385,14 +380,9 @@
         lax.fori_loop(0, 2, columns, 0)
         for n in range(3):
             remote(prod.at[j, n], zgot.at[j, n], z_send.at[j, n], z_sem.at[j, n], me, lax.rem(z + 1 + n, 4)).start()
-
-    for j in range(2):
-        for n in range(3):
-            received(zgot.at[j, n], z_sem.at[j, n])
-        for t in range(8):
-            k, at = 8 * j + t, slice(t * 16, t * 16 + 16)
-            summed[k] = (prod[j, 3, at, :] + zgot[j, 0, at, :]) + (zgot[j, 1, at, :] + zgot[j, 2, at, :])
-            remote(summed.at[k], back.at[k], back_send.at[k], back_sem.at[k], device(OFFSETS[k], 1 - c, -1), z).start()
+        if j:
+            finish(j - 1)
+    finish(3)
 
     out_ref[...] = start_ref[...]
     for k in range(16):
@@ -405,7 +395,7 @@
     for k in range(16):
         sent(packed.at[k], send_sem.at[k])
         sent(summed.at[k], back_send.at[k])
-    for j in range(2):
+    for j in range(4):
         for n in range(3):
             sent(prod.at[j, n], z_send.at[j, n])
 
@@ -433,17 +423,17 @@
             pltpu.VMEM((2, KDIM, 2 * ZCOL), bf16),
             pltpu.VMEM((2, KDIM, 2 * ZCOL), bf16),
             pltpu.VMEM((2, 256, NCOL), f32),
-            pltpu.VMEM((256, KDIM), bf16),
-            pltpu.VMEM((GROUPS, 4, 96, ZCOL), f32),
-            pltpu.VMEM((GROUPS, 3, 96, ZCOL), f32),
-            pltpu.VMEM((GROUPS, 2, 3, ROWS, ZCOL), f32),
+            pltpu.VMEM((128, KDIM), bf16),
+            pltpu.VMEM((STEPS, 4, 48, ZCOL), f32),
+            pltpu.VMEM((STEPS, 3, 48, ZCOL), f32),
+            pltpu.VMEM((STEPS, 3, ROWS, ZCOL), f32),
             pltpu.VMEM((16, 3, ROWS, ZCOL), f32),
-            pltpu.VMEM((GROUPS, 32, NCOL), f32),
-            pltpu.VMEM((GROUPS, 32, NCOL), f32),
+            pltpu.VMEM((STEPS, ROWS, NCOL), f32),
+            pltpu.VMEM((STEPS, ROWS, NCOL), f32),
             pltpu.VMEM((32, 8, 128), f32),
             pltpu.VMEM((32, 8, 128), f32),
             dma, dma((2,)), dma((16, 2)), dma((16, 3)), dma((4,)), dma((4,)), dma((4, 2)), dma((16,)),
-            dma((GROUPS, 3)), dma((GROUPS, 3)), dma((16, 2)), dma((16, 2)), dma((GROUPS,)), dma((GROUPS,)), dma, dma,
+            dma((STEPS, 3)), dma((STEPS, 3)), dma((16, 2)), dma((16, 2)), dma((STEPS,)), dma((STEPS,)), dma, dma,
         ],
         compiler_params=pltpu.CompilerParams(
             collective_id=0, has_side_effects=True, vmem_limit_bytes=64 * 2**20 - 2**17),
@@ -465,12 +455,12 @@
                 pltpu.VMEM((2, KDIM, 2 * ZCOL), bf16),
                 pltpu.VMEM((2, KDIM, 2 * ZCOL), bf16),
                 pltpu.VMEM((2, 256, NCOL), f32),
-                pltpu.VMEM((256, KDIM), bf16),
-                pltpu.VMEM((2, 4, 128, ZCOL), f32),
-                pltpu.VMEM((2, 3, 128, ZCOL), f32),
+                pltpu.VMEM((128, KDIM), bf16),
+                pltpu.VMEM((4, 4, 64, ZCOL), f32),
+                pltpu.VMEM((4, 3, 64, ZCOL), f32),
                 pltpu.VMEM((16, ROWS, ZCOL), f32),
                 pltpu.VMEM((16, ROWS, ZCOL), f32),
-                dma, dma((2,)), dma((16,)), dma((16,)), dma((2, 3)), dma((2, 3)), dma((16,)), dma((16,)),
+                dma, dma((2,)), dma((16,)), dma((16,)), dma((4, 3)), dma((4, 3)), dma((16,)), dma((16,)),
             ],
             compiler_params=pltpu.CompilerParams(
                 collective_id=1, has_side_effects=True, vmem_limit_bytes=60 * 2**20),

time: 127 us -> 121 us (0.953)
  Pallas kernels: 122 us -> 116 us
    pallas_call x1, Pallas kernels: 122 us -> 116 us  [shards(): pl.pallas_call(kernel, out_shape=(jax.ShapeDtypeStruct((OBLK, ROWS, ZCOL)...]
where the time goes in v3:
time: 121 us
  Pallas kernels  116 us (96%)
  local copies, waits for them, and re-layouts  2.74 us (2%)
  other arithmetic  1.42 us (1%)
    pallas_call x1, Pallas kernels, shards(): pl.pallas_call(kernel, out_shape=(jax.ShapeDtypeStruct((OBLK, ROWS, ZCOL)...  116 us

profile of v3, /device:TPU:1, one launch (start us, length us, event | category | flops | bytes accessed | tf_op | source)
XLA Modules:
  0.0 121.2 jit_solution(4858965048758376968)
XLA Ops:
  0.0 0.7 multiply_add_fusion
  0.7 0.8 select_reduce_fusion.1
  1.4 116.3 %shard_map.57 = (f32[4,16,384]{2,1,0:T(8,128)}, f32[8,128]{1,0:T(8,128)}) custom-call(s32[32]{0:T(128)S(1)} %get-tuple-element.33.code0, s32[32]{0:T(128)S(1)} %get-tuple-element.32.code1, s32[32]{0:T(128)S(1)} %get-tuple-element.34.holds, f32[32,16,2304]{2,1,0:T(8,128)} %amp_hbm.1, f32[1,2304,1536]{2,1,0:T(8,128)} %int_hbm.1), custom_call_target="tpu_custom_call" | custom-call | flops 21743271936 | bytes 18874368 | tf_op jit(solution)/shard_map/pallas_call | solution.py:413
  117.8 1.2 slice.3
  119.6 1.5 %copy.13 = f32[4,16,384]{2,1,0:T(8,128)} copy(f32[4,16,384]{2,1,0:T(8,128)} %get-tuple-element.31) | data formatting | bytes 196608
  (1 shorter events, 0.0 us)

commit v4 on v3

--- a/solution.py
+++ b/solution.py
@@ -24,7 +24,7 @@
 )
 STEPS = 16
 LAG = 3
-PROMPT = 13
+PROMPT = 15
 RELAYED, RELAYS = 11, 4
 RELAY_VIA = ((2, 0), (2, 0), (0, 2), (0, 2))
 RELAY_ON = ((0, 1), (0, 3), (1, 0), (3, 0))
@@ -131,6 +131,9 @@
 
     for k in EARLY:
         pack(k)
+    pl.semaphore_wait(barrier, 34)
+    for k in EARLY:
+        send(k)
     left = jnp.int32(0)
     for k in range(16):
         near0, near1, far0, far1 = codes(k)
@@ -141,15 +144,12 @@
         mine = jnp.where(near1 > near0, 1.0, 0.0)
         notes[2 * k] = jnp.where(top, mine, left.astype(jnp.float32))
         notes[2 * k + 1] = jnp.where(top, 1.0 - mine, left.astype(jnp.float32))
-    pl.semaphore_wait(barrier, 34)
     for k in range(16):
         remote(notes.at[2 * k + 1], noted.at[2 * k + 1], note_send, note_sem, device(OFFSETS[k], 1 - c), z).start()
         if k == 0:
             noted[0] = notes[0]
         else:
             remote(notes.at[2 * k], noted.at[2 * k], note_send, note_sem, device(OFFSETS[k], c), z).start()
-    for k in EARLY:
-        send(k)
 
     for i in range(9):
         load_stage(i).wait()

time: 121 us -> 120 us (level)
    pallas_call x1, Pallas kernels: 116 us -> 115 us  [shards(): pl.pallas_call(kernel, out_shape=(jax.ShapeDtypeStruct((OBLK, ROWS, ZCOL)...]
where the time goes in v4:
time: 120 us
  Pallas kernels  115 us (96%)
  local copies, waits for them, and re-layouts  2.74 us (2%)
  other arithmetic  1.42 us (1%)
    pallas_call x1, Pallas kernels, shards(): pl.pallas_call(kernel, out_shape=(jax.ShapeDtypeStruct((OBLK, ROWS, ZCOL)...  115 us

profile of v4, /device:TPU:1, one launch (start us, length us, event | category | flops | bytes accessed | tf_op | source)
XLA Modules:
  0.0 119.9 jit_solution(1295080016247305467)
XLA Ops:
  0.0 0.7 multiply_add_fusion
  0.7 0.8 select_reduce_fusion.1
  1.4 115.1 %shard_map.57 = (f32[4,16,384]{2,1,0:T(8,128)}, f32[8,128]{1,0:T(8,128)}) custom-call(s32[32]{0:T(128)S(1)} %get-tuple-element.33.code0, s32[32]{0:T(128)S(1)} %get-tuple-element.32.code1, s32[32]{0:T(128)S(1)} %get-tuple-element.34.holds, f32[32,16,2304]{2,1,0:T(8,128)} %amp_hbm.1, f32[1,2304,1536]{2,1,0:T(8,128)} %int_hbm.1), custom_call_target="tpu_custom_call" | custom-call | flops 21743271936 | bytes 18874368 | tf_op jit(solution)/shard_map/pallas_call | solution.py:413
  116.5 1.2 slice.3
  118.4 1.5 %copy.13 = f32[4,16,384]{2,1,0:T(8,128)} copy(f32[4,16,384]{2,1,0:T(8,128)} %get-tuple-element.31) | data formatting | bytes 196608
  (1 shorter events, 0.0 us)

commit v5 on v4

--- a/solution.py
+++ b/solution.py
@@ -23,7 +23,7 @@
     (2, 2),
 )
 STEPS = 16
-LAG = 3
+LAG = 4
 PROMPT = 15
 RELAYED, RELAYS = 11, 4
 RELAY_VIA = ((2, 0), (2, 0), (0, 2), (0, 2))

time: 120 us -> 120 us (level)
  no operation moved by 1% of the time
where the time goes in v5:
time: 120 us
  Pallas kernels  115 us (96%)
  local copies, waits for them, and re-layouts  2.74 us (2%)
  other arithmetic  1.42 us (1%)
    pallas_call x1, Pallas kernels, shards(): pl.pallas_call(kernel, out_shape=(jax.ShapeDtypeStruct((OBLK, ROWS, ZCOL)...  115 us

profile of v5, /device:TPU:1, one launch (start us, length us, event | category | flops | bytes accessed | tf_op | source)
XLA Modules:
  0.0 119.8 jit_solution(9885327483696522118)
XLA Ops:
  0.0 0.7 multiply_add_fusion
  0.7 0.8 select_reduce_fusion.1
  1.4 115.0 %shard_map.57 = (f32[4,16,384]{2,1,0:T(8,128)}, f32[8,128]{1,0:T(8,128)}) custom-call(s32[32]{0:T(128)S(1)} %get-tuple-element.33.code0, s32[32]{0:T(128)S(1)} %get-tuple-element.32.code1, s32[32]{0:T(128)S(1)} %get-tuple-element.34.holds, f32[32,16,2304]{2,1,0:T(8,128)} %amp_hbm.1, f32[1,2304,1536]{2,1,0:T(8,128)} %int_hbm.1), custom_call_target="tpu_custom_call" | custom-call | flops 21743271936 | bytes 18874368 | tf_op jit(solution)/shard_map/pallas_call | solution.py:413
  116.4 1.2 slice.3
  118.3 1.5 %copy.13 = f32[4,16,384]{2,1,0:T(8,128)} copy(f32[4,16,384]{2,1,0:T(8,128)} %get-tuple-element.31) | data formatting | bytes 196608
  (1 shorter events, 0.0 us)
